TPU v7x, 512 devices: a whole 4x8x8 slice. The times are simulated.
512 devices in a mesh: row: 32 (over y, x), col: 16 (over z, core).
Axes of the slice: x: 4, y: 8, z: 8, core: 2. Of those that a mesh axis runs over, the one named last changes fastest.
Arguments:
- choi: float32 [4, 8192, 4096], P(None, 'row', 'col'), may hold values from -0.5 to 8, as said below
Outputs:
- factored: float32 [4, 8192, 4096], P(None, 'row', 'col')
Inputs may be any that keep to these rules, and one draw needn't show every extreme that they name: `choi`: the leading 4096 x 4096 block of the matrix is symmetric with a positive diagonal, and its leading 2 * 256 square is positive definite.
All inputs are finite; a program needn't handle non-finite values.
Results may differ from a plain program's by a relative error of at most 0.0001.
Values sent between devices are 32-bit elements; how exact they have to be, the bound alone decides.
No kernel may reach another device: no remote copies, remote signals or barrier semaphores. Data moves between devices by JAX's collectives and lax.ppermute only.
A program may use at most 64 MiB of HBM per device.

v0:
```python
import jax
import jax.numpy as jnp
from jax import lax
from jax.sharding import Mesh
from jax.sharding import PartitionSpec as P

PANELS = 2
ROW = ("row_0", "row_1")
COL = ("col_0", "col_1")
ROW_COL = ("row_0", "row_1", "col_0", "col_1")


def picked(array, axis, root):
    return lax.dynamic_index_in_dim(lax.all_gather(array, axis), root, 0, keepdims=False)


def from_root(array, axes, root):
    array = jnp.where(lax.axis_index(axes) == root, array, jnp.zeros_like(array))
    for axis in axes:
        array = lax.psum(array, axis)
    return array


def factor_tile(diagonal):
    tile_size = diagonal.shape[0]
    identity = jnp.eye(tile_size, dtype=jnp.float32)
    factor = jnp.linalg.cholesky(diagonal)
    inverse = jax.scipy.linalg.solve_triangular(factor, identity, lower=True)
    return (factor, inverse)


def panel_from(blocks, factor, inverse, tile_index, step):
    beneath = jnp.einsum("sij,kj->sik", blocks, inverse, precision=lax.Precision.HIGHEST)
    place = tile_index[:, None, None]
    return jnp.where(place > step, beneath, jnp.where(place == step, factor[None], 0.0))


def body(choi):
    slot_count = choi.shape[0]
    row_count = lax.axis_size(ROW)
    col_count = lax.axis_size(COL)
    my_row = lax.axis_index(ROW)
    my_col = lax.axis_index(COL)
    tile_index = jnp.arange(slot_count, dtype=jnp.int32) * row_count + my_row
    current = choi
    for step in range(PANELS):
        row_tile = current[step // row_count]
        tile_row = picked(row_tile, ROW, step % row_count)
        diagonal = from_root(row_tile, ROW_COL, step % row_count * col_count + step)
        raw_tiles = from_root(current, COL, step)
        factor, inverse = factor_tile(diagonal)
        panel_tiles = panel_from(raw_tiles, factor, inverse, tile_index, step)
        partner = jnp.dot(tile_row.T, inverse.T, precision=lax.Precision.HIGHEST)
        updated = current - jnp.einsum(
            "sij,kj->sik", panel_tiles, partner, precision=lax.Precision.HIGHEST
        )
        trailing = (tile_index[:, None, None] > step) & (my_col > step)
        current = jnp.where(my_col == step, panel_tiles, jnp.where(trailing, updated, current))
    cleared = (my_col >= PANELS) & (tile_index[:, None, None] < PANELS)
    return jnp.where(cleared, 0.0, current)


def solution(mesh):
    finer = Mesh(mesh.devices.reshape(8, 4, 8, 2), ("row_0", "row_1", "col_0", "col_1"))
    placed = (P(None, ROW, COL),)
    return jax.shard_map(
        body, mesh=finer, in_specs=placed, out_specs=P(None, ROW, COL), check_vma=False
    )
```

profile of v0, /device:TPU:1, one launch (start us, length us, event | category | flops | bytes accessed | tf_op | source)
XLA Modules:
  0.0 675.9 jit_solution(7422537290769370134)
XLA Ops:
  7.4 1.6 copy.19
  8.9 0.7 fusion.33
  9.8 79.2 %all-reduce.14.cloned.1.call-done = f32[256,256]{0,1:T(8,128)} async-done(((f32[256,256]{0,1:T(8,128)}), f32[256,256]{0,1:T(8,128)}) %all-reduce.14.cloned.1.call-update) | async-done | bytes 262160 | tf_op jit(solution)/shard_map/psum | solution.py:20
  89.1 1.1 broadcast_select_fusion.1
  90.1 55.0 %all-reduce.16.cloned.1.call-done = f32[256,256]{0,1:T(8,128)} async-done(((f32[256,256]{0,1:T(8,128)}), f32[256,256]{0,1:T(8,128)}) %all-reduce.16.cloned.1.call-update) | async-done | bytes 262160 | tf_op jit(solution)/shard_map/psum | solution.py:20
  145.2 84.3 %all-reduce.24.cloned.1.call-done = (f32[4,256,256]{1,2,0:T(8,128)}, f32[256,256]{0,1:T(8,128)}) async-done(((f32[4,256,256]{1,2,0:T(8,128)}, f32[256,256]{0,1:T(8,128)}), (f32[4,256,256]{1,2,0:T(8,128)}, f32[256,256]{0,1:T(8,128)})) %all-reduce.24.cloned.1.call-update) | async-done | bytes 1310736 | tf_op jit(solution)/shard_map/psum | solution.py:20
  229.6 0.8 copy.25
  230.6 42.0 %all-reduce.28.cloned.1.call-done = (f32[4,256,256]{1,2,0:T(8,128)}, f32[256,256]{0,1:T(8,128)}) async-done(((f32[4,256,256]{1,2,0:T(8,128)}, f32[256,256]{0,1:T(8,128)}), (f32[4,256,256]{1,2,0:T(8,128)}, f32[256,256]{0,1:T(8,128)})) %all-reduce.28.cloned.1.call-update) | async-done | bytes 1310736 | tf_op jit(solution)/shard_map/psum | solution.py:20
  272.6 1.1 copy.21
  273.7 1.0 fusion.6
  274.7 11.7 %cholesky.130 = f32[128,128]{1,0:T(8,128)S(1)} custom-call(f32[128,128]{1,0:T(8,128)S(1)} %cholesky.194), custom_call_target="Cholesky" | custom-call | tf_op jit(solution)/shard_map/jit(cholesky)/cholesky | solution.py:27
  286.5 9.8 %custom-call.13 = f32[1,128,128]{1,2,0:T(8,128)S(1)} custom-call(f32[1,128,128]{2,1,0:T(8,128)S(1)} %get-tuple-element.66), custom_call_target="InvertDiagBlocksLowerTriangular" | custom-call | tf_op jit(solution)/shard_map/jit(cholesky)/cholesky | solution.py:27
  296.8 11.7 %cholesky.147 = f32[128,128]{1,0:T(8,128)S(1)} custom-call(f32[128,128]{1,0:T(8,128)S(1)} %convolution_subtract_fusion.3), custom_call_target="Cholesky" | custom-call | tf_op jit(solution)/shard_map/jit(cholesky)/cholesky | solution.py:27
  308.5 0.7 compare_reduce_fusion.2
  310.6 4.0 while.4
  310.8 0.6 fusion.50
  311.4 1.3 bitcast_dynamic-update-slice_fusion.4
  312.7 0.6 fusion.50
  313.3 1.3 bitcast_dynamic-update-slice_fusion.4
  314.6 19.7 %custom-call.14 = f32[2,128,128]{1,2,0:T(8,128)S(1)} custom-call(f32[2,128,128]{2,1,0:T(8,128)S(1)} %get-tuple-element.21), custom_call_target="InvertDiagBlocksLowerTriangular" | custom-call | tf_op jit(solution)/shard_map/jit(_solve_triangular)/triangular_solve | solution.py:28
  335.2 2.3 convolution_select_fusion.1
  337.5 1.6 all-gather.3.cloned.1.call-done
  339.1 1.3 convolution_bitcast_fusion.1
  340.5 2.3 broadcast_select_fusion
  342.8 0.7 fusion.32
  343.6 71.4 %all-reduce.18.cloned.1.call-done = f32[256,256]{0,1:T(8,128)} async-done(((f32[256,256]{0,1:T(8,128)}), f32[256,256]{0,1:T(8,128)}) %all-reduce.18.cloned.1.call-update) | async-done | bytes 262160 | tf_op jit(solution)/shard_map/psum | solution.py:20
  415.0 55.8 %all-reduce.20.cloned.1.call-done = f32[256,256]{0,1:T(8,128)} async-done(((f32[256,256]{0,1:T(8,128)}), f32[256,256]{0,1:T(8,128)}) %all-reduce.20.cloned.1.call-update) | async-done | bytes 262160 | tf_op jit(solution)/shard_map/psum | solution.py:20
  470.9 84.4 %all-reduce.22.cloned.1.call-done = (f32[4,256,256]{1,2,0:T(8,128)}, f32[256,256]{0,1:T(8,128)}) async-done(((f32[4,256,256]{1,2,0:T(8,128)}, f32[256,256]{0,1:T(8,128)}), (f32[4,256,256]{1,2,0:T(8,128)}, f32[256,256]{0,1:T(8,128)})) %all-reduce.22.cloned.1.call-update) | async-done | bytes 1310736 | tf_op jit(solution)/shard_map/psum | solution.py:20
  555.3 0.8 copy.34
  556.2 42.5 %all-reduce.26.cloned.1.call-done = (f32[4,256,256]{1,2,0:T(8,128)}, f32[256,256]{0,1:T(8,128)}) async-done(((f32[4,256,256]{1,2,0:T(8,128)}, f32[256,256]{0,1:T(8,128)}), (f32[4,256,256]{1,2,0:T(8,128)}, f32[256,256]{0,1:T(8,128)})) %all-reduce.26.cloned.1.call-update) | async-done | bytes 1310736 | tf_op jit(solution)/shard_map/psum | solution.py:20
  598.7 1.1 copy.30
  599.8 1.0 fusion.4
  600.8 11.7 %cholesky.164 = f32[128,128]{1,0:T(8,128)S(1)} custom-call(f32[128,128]{1,0:T(8,128)S(1)} %cholesky.197), custom_call_target="Cholesky" | custom-call | tf_op jit(solution)/shard_map/jit(cholesky)/cholesky | solution.py:27
  612.6 9.8 %custom-call.15 = f32[1,128,128]{1,2,0:T(8,128)S(1)} custom-call(f32[1,128,128]{2,1,0:T(8,128)S(1)} %get-tuple-element.62), custom_call_target="InvertDiagBlocksLowerTriangular" | custom-call | tf_op jit(solution)/shard_map/jit(cholesky)/cholesky | solution.py:27
  622.9 11.7 %cholesky.181 = f32[128,128]{1,0:T(8,128)S(1)} custom-call(f32[128,128]{1,0:T(8,128)S(1)} %convolution_subtract_fusion.2), custom_call_target="Cholesky" | custom-call | tf_op jit(solution)/shard_map/jit(cholesky)/cholesky | solution.py:27
  634.6 0.7 compare_reduce_fusion.1
  635.3 0.6 compare_reduce_fusion
  637.3 4.0 while.5
  637.6 0.6 fusion.51
  638.2 1.3 bitcast_dynamic-update-slice_fusion.5
  639.5 0.6 fusion.51
  640.1 1.3 bitcast_dynamic-update-slice_fusion.5
  641.3 19.7 %custom-call.16 = f32[2,128,128]{1,2,0:T(8,128)S(1)} custom-call(f32[2,128,128]{2,1,0:T(8,128)S(1)} %get-tuple-element.22), custom_call_target="InvertDiagBlocksLowerTriangular" | custom-call | tf_op jit(solution)/shard_map/jit(_solve_triangular)/triangular_solve | solution.py:28
  661.0 0.3 fusion.11
  661.9 2.3 convolution_select_fusion
  664.4 1.5 convolution_bitcast_fusion
  665.9 1.2 fusion.1
  667.1 1.3 copy.37
  (55 shorter events, 3.8 us)
Async XLA Ops:
  7.4 81.6 %all-reduce.14.cloned.1.call-start = ((), (), s32[]{:S(2)}) async-start(), calls=%async_computation | async-start | bytes 524288 | tf_op jit(solution)/shard_map/psum | solution.py:20
  9.7 135.4 %all-reduce.16.cloned.1.call-start = ((), (), s32[]{:S(2)}) async-start(), calls=%async_computation.1 | async-start | bytes 524288 | tf_op jit(solution)/shard_map/psum | solution.py:20
  89.0 140.5 %all-reduce.24.cloned.1.call-start = ((), (), s32[]{:S(2)}) async-start(), calls=%async_computation.7 | async-start | bytes 2621440 | tf_op jit(solution)/shard_map/psum | solution.py:20
  145.2 127.5 %all-reduce.28.cloned.1.call-start = ((), (), s32[]{:S(2)}) async-start(), calls=%async_computation.9 | async-start | bytes 2621440 | tf_op jit(solution)/shard_map/psum | solution.py:20
  229.5 109.6 %all-gather.3.cloned.1.call-start = ((), (), s32[]{:S(2)}) async-start(), calls=%async_computation.2 | async-start | bytes 8650752 | tf_op jit(solution)/shard_map/all_gather | solution.py:14
  230.5 184.5 %all-reduce.18.cloned.1.call-start = ((), (), s32[]{:S(2)}) async-start(), calls=%async_computation.3 | async-start | bytes 524288 | tf_op jit(solution)/shard_map/psum | solution.py:20
  343.5 127.3 %all-reduce.20.cloned.1.call-start = ((), (), s32[]{:S(2)}) async-start(), calls=%async_computation.4 | async-start | bytes 524288 | tf_op jit(solution)/shard_map/psum | solution.py:20
  414.9 140.3 %all-reduce.22.cloned.1.call-start = ((), (), s32[]{:S(2)}) async-start(), calls=%async_computation.6 | async-start | bytes 2621440 | tf_op jit(solution)/shard_map/psum | solution.py:20
  470.8 127.9 %all-reduce.26.cloned.1.call-start = ((), (), s32[]{:S(2)}) async-start(), calls=%async_computation.8 | async-start | bytes 2621440 | tf_op jit(solution)/shard_map/psum | solution.py:20
  555.3 109.1 %all-gather.5.cloned.1.call-start = ((), (), s32[]{:S(2)}) async-start(), calls=%async_computation.5 | async-start | bytes 8650752 | tf_op jit(solution)/shard_map/all_gather | solution.py:14
Sparse Core Ops, SparseCore 0:
  10.5 78.4 all-reduce.13
  91.4 53.6 all-reduce.15
  147.6 81.9 all-reduce.23
  232.3 40.2 all-reduce.27
  343.6 71.2 all-reduce.17
  417.1 53.6 all-reduce.19
  473.4 81.8 all-reduce.21
  558.4 40.2 all-reduce.25
Sparse Core Ops, SparseCore 1:
  233.7 105.4 all-gather.2
  558.9 105.4 all-gather.4
where the time goes:
time: 676 us
  waiting for transfers between devices  517 us (76%)
  other arithmetic  113 us (17%)
  between operations  17.7 us (3%)
  local copies, waits for them, and re-layouts  14.6 us (2%)
  matrix products  13.7 us (2%)
    psum x8, waiting for transfers between devices, from_root(): array = lax.psum(array, axis)  515 us
    another operation x13, other arithmetic, factor_tile(): factor = jnp.linalg.cholesky(diagonal)  68.5 us
    another operation x5, other arithmetic, factor_tile(): inverse = jax.scipy.linalg.solve_triangular(factor, identity, lower=True)  39.4 us
  transfers between devices with their start and end apart: 10, of which 10 were waited for; matrix products, arithmetic and copies ran while one was open for 19% of the time, Pallas kernels for 0%

commit v1 on v0

--- a/solution.py
+++ b/solution.py
@@ -17,7 +17,8 @@
 def from_root(array, axes, root):
     array = jnp.where(lax.axis_index(axes) == root, array, jnp.zeros_like(array))
     for axis in axes:
-        array = lax.psum(array, axis)
+        parts = lax.all_gather(array, axis, axis=0, tiled=False)
+        array = parts.sum(axis=0)
     return array
 
 

time: 676 us -> 728 us (1.077)
  other arithmetic: 113 us -> 138 us
  waiting for transfers between devices: 517 us -> 532 us
  blocking collectives: 0 us -> 13.6 us
    psum x8 -> x0, waiting for transfers between devices: 515 us -> none  [from_root(): array = lax.psum(array, axis)]
    all_gather x0 -> x10, waiting for transfers between devices: none -> 409 us  [from_root(): parts = lax.all_gather(array, axis, axis=0, tiled=False)]
    all_gather x2, waiting for transfers between devices: 1.72 us -> 121 us  [picked(): lax.all_gather(array, axis)]
    reduce_sum x0 -> x12, other arithmetic: none -> 26.4 us  [from_root(): array = parts.sum(axis=0)]
    all_gather x0 -> x2, blocking collectives: none -> 13.6 us  [from_root(): parts = lax.all_gather(array, axis, axis=0, tiled=False)]
  transfers between devices with their start and end apart: 10 -> 12, of which waited for: 10 -> 12; matrix products, arithmetic and copies ran while one was open for 19% -> 19% of each run, Pallas kernels for 0% -> 0%
where the time goes in v1:
time: 728 us; the launch traced here: 721 us
  waiting for transfers between devices  532 us (73%)
  other arithmetic  138 us (19%)
  between operations  16.5 us (2%)
  blocking collectives  13.6 us (2%)
  matrix products  11.6 us (2%)
  local copies, waits for them, and re-layouts  7.96 us (1%)
    all_gather x10, waiting for transfers between devices, from_root(): parts = lax.all_gather(array, axis, axis=0, tiled=False)  409 us
    all_gather x2, waiting for transfers between devices, picked(): lax.all_gather(array, axis)  121 us
    another operation x13, other arithmetic, factor_tile(): factor = jnp.linalg.cholesky(diagonal)  68.5 us
    another operation x5, other arithmetic, factor_tile(): inverse = jax.scipy.linalg.solve_triangular(factor, identity, lower=True)  39.4 us
    reduce_sum x12, other arithmetic, from_root(): array = parts.sum(axis=0)  26.4 us
  transfers between devices with their start and end apart: 12, of which 12 were waited for; matrix products, arithmetic and copies ran while one was open for 19% of the time, Pallas kernels for 0%

profile of v1, /device:TPU:1, one launch (start us, length us, event | category | flops | bytes accessed | tf_op | source)
XLA Modules:
  0.0 721.1 jit_solution(4719541552113364527)
XLA Ops:
  6.5 1.8 fusion.33
  8.4 46.5 %all-gather.23.cloned.1.call-done = f32[8,256,256]{2,1,0:T(8,128)} async-done(((f32[1,256,256]{2,1,0:T(8,128)}), f32[8,256,256]{2,1,0:T(8,128)}) %all-gather.23.cloned.1.call-update) | async-done | bytes 2097168 | tf_op jit(solution)/shard_map/all_gather | solution.py:20
  54.9 2.5 reduce_sum.110
  57.4 31.3 %all-gather.35.cloned.1.call-done = f32[1024,256]{1,0:T(8,128)} async-done(((f32[256,256]{1,0:T(8,128)}), f32[1024,256]{1,0:T(8,128)}) %all-gather.35.cloned.1.call-update) | async-done | bytes 1048592 | tf_op jit(solution)/shard_map/all_gather | solution.py:20
  88.7 2.0 reduce_sum.111
  90.8 1.1 broadcast_select_fusion.1
  92.6 40.1 %all-gather.37.cloned.1.call-done = f32[2048,256]{1,0:T(8,128)} async-done(((f32[256,256]{1,0:T(8,128)}), f32[2048,256]{1,0:T(8,128)}) %all-gather.37.cloned.1.call-update) | async-done | bytes 2097168 | tf_op jit(solution)/shard_map/all_gather | solution.py:20
  132.8 1.8 reduce_sum.112
  134.5 6.5 all-gather.4
  141.3 11.7 %cholesky.130 = f32[128,128]{1,0:T(8,128)S(1)} custom-call(f32[128,128]{1,0:T(8,128)S(1)} %cholesky.194), custom_call_target="Cholesky" | custom-call | tf_op jit(solution)/shard_map/jit(cholesky)/cholesky | solution.py:28
  153.1 9.8 %custom-call.13 = f32[1,128,128]{1,2,0:T(8,128)S(1)} custom-call(f32[1,128,128]{2,1,0:T(8,128)S(1)} %get-tuple-element.58), custom_call_target="InvertDiagBlocksLowerTriangular" | custom-call | tf_op jit(solution)/shard_map/jit(cholesky)/cholesky | solution.py:28
  163.1 71.4 %all-gather.31.cloned.1.call-done = f32[32,256,256]{2,1,0:T(8,128)} async-done(((f32[4,256,256]{2,1,0:T(8,128)}), f32[32,256,256]{2,1,0:T(8,128)}) %all-gather.31.cloned.1.call-update) | async-done | bytes 8388624 | tf_op jit(solution)/shard_map/all_gather | solution.py:20
  234.5 5.1 reduce_sum.108
  240.2 11.7 %cholesky.147 = f32[128,128]{1,0:T(8,128)S(1)} custom-call(f32[128,128]{1,0:T(8,128)S(1)} %convolution_subtract_fusion.3), custom_call_target="Cholesky" | custom-call | tf_op jit(solution)/shard_map/jit(cholesky)/cholesky | solution.py:28
  254.0 3.8 while.4
  254.6 1.3 bitcast_dynamic-update-slice_fusion.4
  256.5 1.3 bitcast_dynamic-update-slice_fusion.4
  257.8 19.7 %custom-call.14 = f32[2,128,128]{1,2,0:T(8,128)S(1)} custom-call(f32[2,128,128]{2,1,0:T(8,128)S(1)} %get-tuple-element.21), custom_call_target="InvertDiagBlocksLowerTriangular" | custom-call | tf_op jit(solution)/shard_map/jit(_solve_triangular)/triangular_solve | solution.py:29
  278.4 60.7 %all-gather.25.cloned.1.call-done = f32[32,256,256]{2,1,0:T(8,128)} async-done(((f32[1,256,256]{2,1,0:T(8,128)}), f32[32,256,256]{2,1,0:T(8,128)}) %all-gather.25.cloned.1.call-update) | async-done | bytes 8388624 | tf_op jit(solution)/shard_map/all_gather | solution.py:14
  339.1 1.3 convolution_bitcast_fusion.1
  340.4 18.8 %all-gather.33.cloned.1.call-done = f32[8,256,256]{2,1,0:T(8,128)} async-done(((f32[4,256,256]{2,1,0:T(8,128)}), f32[8,256,256]{2,1,0:T(8,128)}) %all-gather.33.cloned.1.call-update) | async-done | bytes 2097168 | tf_op jit(solution)/shard_map/all_gather | solution.py:20
  359.2 1.9 reduce_sum.109
  361.0 1.1 convolution_select_fusion.1
  362.1 2.0 broadcast_select_fusion
  364.1 0.9 fusion.32
  365.1 39.9 %all-gather.27.cloned.1.call-done = f32[8,256,256]{2,1,0:T(8,128)} async-done(((f32[1,256,256]{2,1,0:T(8,128)}), f32[8,256,256]{2,1,0:T(8,128)}) %all-gather.27.cloned.1.call-update) | async-done | bytes 2097168 | tf_op jit(solution)/shard_map/all_gather | solution.py:20
  404.9 2.5 reduce_sum.116
  407.5 31.3 %all-gather.43.cloned.1.call-done = f32[1024,256]{1,0:T(8,128)} async-done(((f32[256,256]{1,0:T(8,128)}), f32[1024,256]{1,0:T(8,128)}) %all-gather.43.cloned.1.call-update) | async-done | bytes 1048592 | tf_op jit(solution)/shard_map/all_gather | solution.py:20
  438.8 2.0 reduce_sum.117
  441.5 0.7 all-gather.29.cloned.1.call-update
  442.2 40.6 %all-gather.45.cloned.1.call-done = f32[2048,256]{1,0:T(8,128)} async-done(((f32[256,256]{1,0:T(8,128)}), f32[2048,256]{1,0:T(8,128)}) %all-gather.45.cloned.1.call-update) | async-done | bytes 2097168 | tf_op jit(solution)/shard_map/all_gather | solution.py:20
  482.9 1.8 reduce_sum.118
  484.6 7.0 all-gather.9
  491.9 11.7 %cholesky.164 = f32[128,128]{1,0:T(8,128)S(1)} custom-call(f32[128,128]{1,0:T(8,128)S(1)} %cholesky.197), custom_call_target="Cholesky" | custom-call | tf_op jit(solution)/shard_map/jit(cholesky)/cholesky | solution.py:28
  503.6 9.8 %custom-call.15 = f32[1,128,128]{1,2,0:T(8,128)S(1)} custom-call(f32[1,128,128]{2,1,0:T(8,128)S(1)} %get-tuple-element.54), custom_call_target="InvertDiagBlocksLowerTriangular" | custom-call | tf_op jit(solution)/shard_map/jit(cholesky)/cholesky | solution.py:28
  513.9 70.8 %all-gather.39.cloned.1.call-done = f32[32,256,256]{2,1,0:T(8,128)} async-done(((f32[4,256,256]{2,1,0:T(8,128)}), f32[32,256,256]{2,1,0:T(8,128)}) %all-gather.39.cloned.1.call-update) | async-done | bytes 8388624 | tf_op jit(solution)/shard_map/all_gather | solution.py:20
  584.7 5.0 reduce_sum.114
  590.4 11.7 %cholesky.181 = f32[128,128]{1,0:T(8,128)S(1)} custom-call(f32[128,128]{1,0:T(8,128)S(1)} %convolution_subtract_fusion.2), custom_call_target="Cholesky" | custom-call | tf_op jit(solution)/shard_map/jit(cholesky)/cholesky | solution.py:28
  604.0 4.0 while.5
  604.8 1.3 bitcast_dynamic-update-slice_fusion.5
  606.7 1.3 bitcast_dynamic-update-slice_fusion.5
  608.0 19.7 %custom-call.16 = f32[2,128,128]{1,2,0:T(8,128)S(1)} custom-call(f32[2,128,128]{2,1,0:T(8,128)S(1)} %get-tuple-element.22), custom_call_target="InvertDiagBlocksLowerTriangular" | custom-call | tf_op jit(solution)/shard_map/jit(_solve_triangular)/triangular_solve | solution.py:29
  628.6 60.4 %all-gather.29.cloned.1.call-done = f32[32,256,256]{2,1,0:T(8,128)} async-done(((f32[1,256,256]{2,1,0:T(8,128)}), f32[32,256,256]{2,1,0:T(8,128)}) %all-gather.29.cloned.1.call-update) | async-done | bytes 8388624 | tf_op jit(solution)/shard_map/all_gather | solution.py:14
  689.0 1.5 convolution_bitcast_fusion
  690.6 18.6 %all-gather.41.cloned.1.call-done = f32[8,256,256]{2,1,0:T(8,128)} async-done(((f32[4,256,256]{2,1,0:T(8,128)}), f32[8,256,256]{2,1,0:T(8,128)}) %all-gather.41.cloned.1.call-update) | async-done | bytes 2097168 | tf_op jit(solution)/shard_map/all_gather | solution.py:20
  709.1 1.9 reduce_sum.115
  711.0 1.0 convolution_select_fusion
  712.0 2.0 fusion.1
  (71 shorter events, 9.8 us)
Async XLA Ops:
  6.5 48.3 %all-gather.23.cloned.1.call-start = ((), (), s32[]{:S(2)}) async-start(), calls=%async_computation | async-start | bytes 2359296 | tf_op jit(solution)/shard_map/all_gather | solution.py:20
  8.3 80.4 %all-gather.35.cloned.1.call-start = ((), (), s32[]{:S(2)}) async-start(), calls=%async_computation.6 | async-start | bytes 1310720 | tf_op jit(solution)/shard_map/all_gather | solution.py:20
  57.3 75.4 %all-gather.37.cloned.1.call-start = ((), (), s32[]{:S(2)}) async-start(), calls=%async_computation.7 | async-start | bytes 2359296 | tf_op jit(solution)/shard_map/all_gather | solution.py:20
  90.8 143.8 %all-gather.31.cloned.1.call-start = ((), (), s32[]{:S(2)}) async-start(), calls=%async_computation.4 | async-start | bytes 9437184 | tf_op jit(solution)/shard_map/all_gather | solution.py:20
  91.9 247.2 %all-gather.25.cloned.1.call-start = ((), (), s32[]{:S(2)}) async-start(), calls=%async_computation.1 | async-start | bytes 8650752 | tf_op jit(solution)/shard_map/all_gather | solution.py:14
  92.5 266.7 %all-gather.33.cloned.1.call-start = ((), (), s32[]{:S(2)}) async-start(), calls=%async_computation.5 | async-start | bytes 3145728 | tf_op jit(solution)/shard_map/all_gather | solution.py:20
  234.5 127.6 %copy-start = (f32[4,256,256]{2,1,0:T(8,128)S(1)}, f32[4,256,256]{2,1,0:T(8,128)}, u32[]{:S(2)}) copy-start(f32[4,256,256]{2,1,0:T(8,128)} %param.4) | copy-start | bytes 3145732
  239.7 165.2 %all-gather.27.cloned.1.call-start = ((), (), s32[]{:S(2)}) async-start(), calls=%async_computation.2 | async-start | bytes 2359296 | tf_op jit(solution)/shard_map/all_gather | solution.py:20
  365.0 73.8 %all-gather.43.cloned.1.call-start = ((), (), s32[]{:S(2)}) async-start(), calls=%async_computation.10 | async-start | bytes 1310720 | tf_op jit(solution)/shard_map/all_gather | solution.py:20
  407.4 75.4 %all-gather.45.cloned.1.call-start = ((), (), s32[]{:S(2)}) async-start(), calls=%async_computation.11 | async-start | bytes 2359296 | tf_op jit(solution)/shard_map/all_gather | solution.py:20
  440.8 143.9 %all-gather.39.cloned.1.call-start = ((), (), s32[]{:S(2)}) async-start(), calls=%async_computation.8 | async-start | bytes 9437184 | tf_op jit(solution)/shard_map/all_gather | solution.py:20
  441.4 247.6 %all-gather.29.cloned.1.call-start = ((), (), s32[]{:S(2)}) async-start(), calls=%async_computation.3 | async-start | bytes 8650752 | tf_op jit(solution)/shard_map/all_gather | solution.py:14
  442.2 267.0 %all-gather.41.cloned.1.call-start = ((), (), s32[]{:S(2)}) async-start(), calls=%async_computation.9 | async-start | bytes 3145728 | tf_op jit(solution)/shard_map/all_gather | solution.py:20
Sparse Core Ops, SparseCore 0:
  9.4 45.3 all-gather.22
  57.5 31.1 all-gather.34
  90.9 41.8 all-gather.36
  134.7 99.7 all-gather.30
  237.5 101.4 all-gather.24
  341.0 18.1 all-gather.32
  365.1 39.7 all-gather.26
  407.5 31.1 all-gather.42
  440.9 41.8 all-gather.44
  484.8 99.8 all-gather.38
  587.9 101.1 all-gather.28
  691.0 18.1 all-gather.40
